TPU v7x, 512 devices: a whole 4x8x8 slice. The times are simulated.
512 devices in a mesh: dp: 8 (over x, core), ctx: 64 (over y, z).
Axes of the slice: x: 4, y: 8, z: 8, core: 2. Of those that a mesh axis runs over, the one named last changes fastest.
Arguments:
- token_ids: int32 [8, 8192], P('dp', 'ctx'), may hold values from 0 to 7
- queries: bfloat16 [8, 8192, 4096], P('dp', 'ctx'), may hold values from -6 to 6
- gated_values: bfloat16 [8, 8192, 4096], P('dp', 'ctx'), may hold values from -6 to 6
- out_grad: bfloat16 [8, 8192, 4096], P('dp', 'ctx'), may hold values from -6 to 6
- filters: bfloat16 [4096, 128], P('ctx'), may hold values from -0.5 to 0.5
Outputs:
- value_grad: bfloat16 [8, 8192, 4096], P('dp', 'ctx')
- filter_grad: float32 [4096, 128], P('ctx')
Inputs may be any that keep to these rules, and one draw needn't show every extreme that they name: `token_ids`: ids 0 to 3 are upper-case bases, 4 to 7 lower-case bases.
All inputs are finite; a program needn't handle non-finite values.
Results may differ from a plain program's by a relative error of at most 0.0049.
Values may be sent and summed in bfloat16 or wider, within the bound.
A program may use at most 64 MiB of HBM per device.

v0:
```python
import functools

import jax
import jax.numpy as jnp
import numpy as np
from jax import lax
from jax.experimental import pallas as pl
from jax.experimental.pallas import tpu as pltpu
from jax.sharding import PartitionSpec as P

F32, BF16 = jnp.float32, jnp.bfloat16
SIDES = {64: (8, 8)}


def tables(rows):
    span = 2 * rows
    angle = np.pi * (2 * np.arange(rows)[:, None] + 1) * np.arange(span)[None, :] / span
    wave = np.concatenate([np.cos(angle), np.sin(angle)], axis=0)
    high = wave.astype(BF16)
    low = (wave - high.astype(np.float64)).astype(BF16)
    own = np.concatenate([high[:, :rows], low[:, :rows]], axis=1)
    after = np.concatenate([high[:, rows:], low[:, rows:]], axis=1)
    back = np.concatenate([high[:, :rows].T, low[:, :rows].T], axis=0)
    back = (back.astype(np.float64) / rows).astype(BF16)
    return np.concatenate([own, after, back], axis=0)


def mul(a, b):
    return jnp.dot(a, b, preferred_element_type=F32)


def twice(x):
    return jnp.concatenate([x, x], axis=0)


def kernel(
    nx, ny, nz, scale,
    tok, q_hbm, gv_hbm, og_hbm, filt_hbm, tab_hbm,
    v_hbm, g_hbm,
    q_v, og_v, gv_v, tab, w_v, cot, halo, cspec, gspec, fbuf, v_v,
    gst, r0, s0, r1, s1, r2, s2, r3, fg,
    lsem, osem, ssem, rsem,
):
    rows = q_v.shape[0]
    chunks = nz // 2
    pairs = ny // 2
    dp, ctx = lax.axis_index("dp"), lax.axis_index("ctx")
    x, c = dp // 2, dp % 2
    y, z = ctx // nz, ctx % nz
    nctx, ndp = ny * nz, 2 * nx
    part = 64 // ndp
    frows = pl.ds(pl.multiple_of(x * (64 // nx), 16), 64 // nx)

    barrier = pltpu.get_barrier_semaphore()
    peers = [{"ctx": (ctx + 1) % nctx}, {"ctx": (ctx + nctx - 1) % nctx}]
    peers += [{"dp": (dp + d) % ndp} for d in range(1, ndp)]
    peers += [{"ctx": ((y + d) % ny) * nz + z} for d in range(1, ny)]
    peers += [{"ctx": y * nz + (z + d) % nz} for d in range(1, nz)]
    for peer in peers:
        pl.semaphore_signal(barrier, inc=1, device_id=peer, device_id_type=pl.DeviceIdType.MESH)

    loads = [
        pltpu.make_async_copy(q_hbm, q_v, lsem.at[0]),
        pltpu.make_async_copy(og_hbm, og_v, lsem.at[1]),
        pltpu.make_async_copy(filt_hbm.at[frows], fbuf.at[y, z, frows], lsem.at[2]),
        pltpu.make_async_copy(tab_hbm, tab, lsem.at[3]),
        pltpu.make_async_copy(gv_hbm, gv_v, lsem.at[4]),
    ]
    for load in loads:
        load.start()

    started = []

    def send(src, dst, **where):
        n = len(started)
        copy = pltpu.make_async_remote_copy(
            src_ref=src, dst_ref=dst, send_sem=ssem.at[n], recv_sem=rsem.at[n],
            device_id=where, device_id_type=pl.DeviceIdType.MESH,
        )
        copy.start()
        started.append(copy)
        return copy

    def arrive(copies):
        for copy in copies:
            copy.wait_recv()

    def cols(p, i):
        return pl.ds(pl.multiple_of(i * (nz * 64) + p * 128, 128), 128)

    weight = jnp.where(tok[...] < 4, 1.0, 0.1).astype(F32)
    w_v[...] = jnp.broadcast_to(weight, (rows, rows)).T

    def make_cot(p):
        @pl.loop(0, ny)
        def _(i):
            at = cols(p, i)
            cot[p, i] = (w_v[...] * og_v[:, at].astype(F32) * q_v[:, at].astype(F32)).astype(BF16)

    def send_halo(p):
        return send(cot.at[p], halo.at[p], ctx=(ctx + nctx - 1) % nctx)

    own, after = pl.ds(0, 2 * rows), pl.ds(2 * rows, 2 * rows)
    back, back_high = pl.ds(4 * rows, 2 * rows), pl.ds(4 * rows, rows)

    def correlate(wave, other):
        a, b = wave[:rows], wave[rows:]
        e, f = other[:rows], other[rows:]
        both = jnp.concatenate([a * e + b * f, b * e - a * f], axis=0)
        top = both.astype(BF16)
        rest = (both - top.astype(F32)).astype(BF16)
        full = mul(tab[back, :], top)
        return full[:rows] + full[rows:] + mul(tab[back_high, :], rest)

    def spectra(p):
        @pl.loop(0, pairs)
        def _(k):
            cspec[p, k] = mul(tab[own, :], twice(jnp.concatenate([cot[p, 2 * k], cot[p, 2 * k + 1]], axis=1)))
            gv = jnp.concatenate([gv_v[:, cols(p, 2 * k)], gv_v[:, cols(p, 2 * k + 1)]], axis=1)
            gspec[p, k] = mul(tab[own, :], twice(gv))

    live = jnp.where(ctx == nctx - 1, 0.0, 1.0).astype(F32)

    def tap_sums(p):
        @pl.loop(0, pairs)
        def _(k):
            far = mul(tab[after, :], twice(jnp.concatenate([halo[p, 2 * k], halo[p, 2 * k + 1]], axis=1)))
            wave = cspec[p, k] + live * far
            cspec[p, k] = wave
            taps = correlate(wave, gspec[p, k])
            for h in range(2):
                turned = taps[:, 128 * h:128 * (h + 1)].T
                for zz in range(2):
                    for xi in range(nx):
                        for ci in range(2):
                            at = zz * 64 + (2 * xi + ci) * part
                            gst[p, ci, xi, 2 * k + h, zz] = turned[at:at + part]

    def values(p):
        @pl.loop(0, pairs)
        def _(k):
            f = jnp.concatenate(
                [fbuf[2 * k + h, 2 * p + zz] for h in range(2) for zz in range(2)], axis=0
            )
            fwave = lax.dot_general(
                tab[own, :], jnp.concatenate([f, f], axis=1), (((1,), (1,)), ((), ())),
                preferred_element_type=F32,
            )
            out = correlate(cspec[p, k], fwave).astype(BF16)
            for h in range(2):
                v_v[:, cols(p, 2 * k + h)] = out[:, 128 * h:128 * (h + 1)]

        stores = []
        for i in range(ny):
            at = cols(p, i)
            stores.append(pltpu.make_async_copy(v_v.at[:, at], v_hbm.at[:, at], osem.at[p, i]))
            stores[-1].start()
        return stores

    def pair_stage(p):
        return [send(gst.at[p, 1 - c], r0.at[p], dp=2 * x + 1 - c)]

    def x_stage(p):
        for xi in range(nx):
            s0[p, xi] = gst[p, c, xi] + r0[p, xi]
        return [
            send(s0.at[p, (x + d) % nx], r1.at[p, d - 1], dp=2 * ((x + d) % nx) + c)
            for d in range(1, nx)
        ]

    def y_stage(p):
        total = s0[p, x]
        for d in range(1, nx):
            total = total + r1[p, d - 1]
        s1[p] = total
        return [
            send(s1.at[p, (y + d) % ny], r2.at[p, d - 1], ctx=((y + d) % ny) * nz + z)
            for d in range(1, ny)
        ]

    def y_total(p):
        total = s1[p, y]
        for d in range(1, ny):
            total = total + r2[p, d - 1]
        s2[p] = total

    loads[0].wait()
    loads[1].wait()
    make_cot(0)
    loads[2].wait()
    pl.semaphore_wait(barrier, len(peers))

    halos = [send_halo(0)]
    fz = [
        send(fbuf.at[y, z, frows], fbuf.at[y, z, frows], ctx=y * nz + (z + d) % nz)
        for d in range(1, nz)
    ]
    for p in range(1, chunks):
        make_cot(p)
        halos.append(send_halo(p))
    loads[3].wait()
    loads[4].wait()
    spectra(0)
    arrive(fz)
    fy = [
        send(fbuf.at[y, :, frows], fbuf.at[y, :, frows], ctx=((y + d) % ny) * nz + z)
        for d in range(1, ny)
    ]
    for p in range(1, chunks):
        spectra(p)

    xs, ys, stores = {}, {}, []
    for p in range(chunks):
        arrive([halos[p]])
        tap_sums(p)
        first = pair_stage(p)
        if p == 0:
            arrive(fy)
            fx = [
                send(fbuf.at[:, :, frows], fbuf.at[:, :, frows], dp=2 * ((x + d) % nx) + c)
                for d in range(1, nx)
            ]
        else:
            arrive(xs[p - 1])
            ys[p - 1] = y_stage(p - 1)
        arrive(first)
        xs[p] = x_stage(p)
        if p == chunks - 2:
            arrive(fx)
            stores += values(0)
    last = chunks - 1
    if chunks == 1:
        arrive(fx)
        stores += values(0)
    if chunks > 1:
        stores += values(1)
    arrive(xs[last])
    ys[last] = y_stage(last)
    for p in range(2, chunks - 1):
        stores += values(p)
    for p in range(chunks):
        arrive(ys[p])
        y_total(p)
    zs = []
    for d in range(1, nz):
        zi = (z + d) % nz
        zs.append(send(s2.at[zi // 2, zi % 2], r3.at[d - 1], ctx=y * nz + zi))
    if chunks > 2:
        stores += values(last)
    arrive(zs)
    total = s2[z // 2, z % 2]
    for d in range(1, nz):
        total = total + r3[d - 1]
    fg[dp] = total * scale
    ds = [send(fg.at[dp], fg.at[dp], dp=(dp + d) % ndp) for d in range(1, ndp)]
    arrive(ds)
    result = pltpu.make_async_copy(fg, g_hbm, lsem.at[5])
    result.start()
    for copy in started:
        copy.wait_send()
    for store in stores:
        store.wait()
    result.wait()


def body(token_ids, queries, gated_values, out_grad, filters):
    ndp, nctx = lax.axis_size("dp"), lax.axis_size("ctx")
    ny, nz = SIDES[nctx]
    nx = ndp // 2
    _, rows, wide = queries.shape
    assert wide == 64 * nctx and rows == 128
    chunks, pairs, part = nz // 2, ny // 2, 64 // ndp
    scale = float(ndp * nctx * rows) ** (-0.5)
    any_space = pl.BlockSpec(memory_space=pl.ANY)
    remote = (nz // 2) * (1 + 1 + (nx - 1) + (ny - 1)) + 2 * (nz - 1) + (ny - 1) + (nx - 1) + (ndp - 1)
    value_grad, filter_grad = pl.pallas_call(
        functools.partial(kernel, nx, ny, nz, scale),
        out_shape=(
            jax.ShapeDtypeStruct((rows, wide), BF16),
            jax.ShapeDtypeStruct((ndp, part, rows), F32),
        ),
        in_specs=[pl.BlockSpec(memory_space=pltpu.VMEM)] + [any_space] * 5,
        out_specs=(any_space, any_space),
        scratch_shapes=[
            pltpu.VMEM((rows, wide), BF16),
            pltpu.VMEM((rows, wide), BF16),
            pltpu.VMEM((rows, wide), BF16),
            pltpu.VMEM((6 * rows, 2 * rows), BF16),
            pltpu.VMEM((rows, rows), F32),
            pltpu.VMEM((chunks, ny, rows, 128), BF16),
            pltpu.VMEM((chunks, ny, rows, 128), BF16),
            pltpu.VMEM((chunks, pairs, 2 * rows, 256), F32),
            pltpu.VMEM((chunks, pairs, 2 * rows, 256), F32),
            pltpu.VMEM((ny, nz, 64, rows), BF16),
            pltpu.VMEM((rows, wide), BF16),
            pltpu.VMEM((chunks, 2, nx, ny, 2, part, rows), F32),
            pltpu.VMEM((chunks, nx, ny, 2, part, rows), F32),
            pltpu.VMEM((chunks, nx, ny, 2, part, rows), F32),
            pltpu.VMEM((chunks, max(nx - 1, 1), ny, 2, part, rows), F32),
            pltpu.VMEM((chunks, ny, 2, part, rows), F32),
            pltpu.VMEM((chunks, ny - 1, 2, part, rows), F32),
            pltpu.VMEM((chunks, 2, part, rows), F32),
            pltpu.VMEM((nz - 1, part, rows), F32),
            pltpu.VMEM((ndp, part, rows), F32),
            pltpu.SemaphoreType.DMA((6,)),
            pltpu.SemaphoreType.DMA((chunks, ny)),
            pltpu.SemaphoreType.DMA((remote,)),
            pltpu.SemaphoreType.DMA((remote,)),
        ],
        compiler_params=pltpu.CompilerParams(
            collective_id=0, has_side_effects=True, vmem_limit_bytes=48 * 1024 * 1024
        ),
        name="mixer_backward",
    )(
        token_ids, queries[0], gated_values[0], out_grad[0], filters, jnp.asarray(tables(rows)),
    )
    return value_grad[None], filter_grad.reshape(64, rows)


def solution(mesh):
    return jax.shard_map(
        body,
        mesh=mesh,
        in_specs=(
            P("dp", "ctx"),
            P("dp", "ctx", None),
            P("dp", "ctx", None),
            P("dp", "ctx", None),
            P("ctx", None),
        ),
        out_specs=(P("dp", "ctx", None), P("ctx", None)),
        check_vma=False,
    )
```

profile of v0, /device:TPU:1, one launch (start us, length us, event | category | flops | bytes accessed | tf_op | source)
XLA Modules:
  0.0 97.4 jit_solution(6455737350146384231)
XLA Ops:
  0.6 0.0 copy-start.5
  0.6 0.6 copy-done.5
  1.3 0.0 copy-start
  1.3 1.2 %copy-done = bf16[1,128,4096]{2,1,0:T(8,128)(2,1)S(1)} copy-done((bf16[1,128,4096]{2,1,0:T(8,128)(2,1)S(1)}, bf16[1,128,4096]{2,1,0:T(8,128)(2,1)}, u32[]{:S(2)}) %copy-start) | copy-done | bytes 1048600
  2.5 0.0 copy-start.1
  2.5 1.2 %copy-done.1 = bf16[1,128,4096]{2,1,0:T(8,128)(2,1)S(1)} copy-done((bf16[1,128,4096]{2,1,0:T(8,128)(2,1)S(1)}, bf16[1,128,4096]{2,1,0:T(8,128)(2,1)}, u32[]{:S(2)}) %copy-start.1) | copy-done | bytes 1048600
  3.7 0.0 copy-start.2
  3.7 1.2 %copy-done.2 = bf16[1,128,4096]{2,1,0:T(8,128)(2,1)S(1)} copy-done((bf16[1,128,4096]{2,1,0:T(8,128)(2,1)S(1)}, bf16[1,128,4096]{2,1,0:T(8,128)(2,1)}, u32[]{:S(2)}) %copy-start.2) | copy-done | bytes 1048600
  5.0 0.0 copy-start.3
  5.0 1.0 %copy-done.3 = bf16[768,256]{1,0:T(8,128)(2,1)S(1)} copy-done((bf16[768,256]{1,0:T(8,128)(2,1)S(1)}, bf16[768,256]{1,0:T(8,128)(2,1)}, u32[]{:S(2)}) %copy-start.3) | copy-done | bytes 393240
  6.0 0.0 copy-start.4
  6.0 0.7 copy-done.4
  6.7 89.1 %mixer_backward.1 = (bf16[128,4096]{1,0:T(8,128)(2,1)S(1)}, f32[8,8,128]{2,1,0:T(8,128)S(1)}) custom-call(s32[1,128]{1,0:T(1,128)S(1)} %copy-done.5, bf16[128,4096]{1,0:T(8,128)(2,1)S(1)} %bitcast.6, bf16[128,4096]{1,0:T(8,128)(2,1)S(1)} %bitcast.7, bf16[128,4096]{1,0:T(8,128)(2,1)S(1)} %bitcast.8, bf16[64,128]{1,0:T(8,128)(2,1)S(1)} %copy-done.4, ...), custom_call_target="tpu_custom_call" | custom-call | tf_op jit(solution)/shard_map/mixer_backward/pallas_call | solution.py:276
  95.8 1.0 copy.10
  96.8 0.6 copy.11
Async XLA Ops:
  0.6 0.7 copy-start.5
  1.3 1.2 %copy-start = (bf16[1,128,4096]{2,1,0:T(8,128)(2,1)S(1)}, bf16[1,128,4096]{2,1,0:T(8,128)(2,1)}, u32[]{:S(2)}) copy-start(bf16[1,128,4096]{2,1,0:T(8,128)(2,1)} %param.7) | copy-start | bytes 3145732
  2.5 1.2 %copy-start.1 = (bf16[1,128,4096]{2,1,0:T(8,128)(2,1)S(1)}, bf16[1,128,4096]{2,1,0:T(8,128)(2,1)}, u32[]{:S(2)}) copy-start(bf16[1,128,4096]{2,1,0:T(8,128)(2,1)} %param.8) | copy-start | bytes 3145732
  3.7 1.2 %copy-start.2 = (bf16[1,128,4096]{2,1,0:T(8,128)(2,1)S(1)}, bf16[1,128,4096]{2,1,0:T(8,128)(2,1)}, u32[]{:S(2)}) copy-start(bf16[1,128,4096]{2,1,0:T(8,128)(2,1)} %param.9) | copy-start | bytes 3145732
  5.0 1.0 %copy-start.3 = (bf16[768,256]{1,0:T(8,128)(2,1)S(1)}, bf16[768,256]{1,0:T(8,128)(2,1)}, u32[]{:S(2)}) copy-start(bf16[768,256]{1,0:T(8,128)(2,1)} %constant.2.clone.tab_hbm) | copy-start | bytes 1179652
  6.0 0.7 copy-start.4
where the time goes:
time: 97.7 us; the launch traced here: 97.4 us
  Pallas kernels  89.1 us (91%)
  local copies, waits for them, and re-layouts  7.62 us (8%)
    pallas_call x1, Pallas kernels, body(): pl.pallas_call(functools.partial(kernel, nx, ny, nz, scale), out_shape=(j...  89.1 us
    unnamed x14, local copies, waits for them, and re-layouts  7.62 us

commit v1 on v0

v1 whole, which is shorter than its diff:
```python
import functools

import jax
import jax.numpy as jnp
import numpy as np
from jax import lax
from jax.experimental import pallas as pl
from jax.experimental.pallas import tpu as pltpu
from jax.sharding import PartitionSpec as P

F32, BF16 = jnp.float32, jnp.bfloat16
SIDES = {64: (8, 8)}


def tables(rows):
    span = 2 * rows
    angle = np.pi * (2 * np.arange(rows)[:, None] + 1) * np.arange(span)[None, :] / span
    wave = np.concatenate([np.cos(angle), np.sin(angle)], axis=0)
    high = wave.astype(BF16)
    low = (wave - high.astype(np.float64)).astype(BF16)
    own = np.concatenate([high[:, :rows], low[:, :rows]], axis=1)
    after = np.concatenate([high[:, rows:], low[:, rows:]], axis=1)
    back = np.concatenate([high[:, :rows].T, low[:, :rows].T], axis=0)
    back = (back.astype(np.float64) / rows).astype(BF16)
    return np.concatenate([own, after, back], axis=0)


def mul(a, b):
    return jnp.dot(a, b, preferred_element_type=F32)


def twice(x):
    return jnp.concatenate([x, x], axis=0)


def kernel(
    nx, ny, nz, scale,
    tok, q_hbm, gv_hbm, og_hbm, filt_hbm, tab_hbm,
    v_hbm, g_hbm,
    q_v, og_v, gv_v, tab, w_v, cot, halo, gv_own, gv_in, cspec, gspec, fin, fbuf, v_v,
    gst, r0, s0, r2, s2, r3, fg, g_v,
    lsem, osem, ssem, rsem,
):
    rows = q_v.shape[0]
    chunks = nz // 2
    pairs = ny // 2
    dp, ctx = lax.axis_index("dp"), lax.axis_index("ctx")
    x, c = dp // 2, dp % 2
    y, z = ctx // nz, ctx % nz
    nctx, ndp = ny * nz, 2 * nx
    frows = pl.ds(pl.multiple_of(x * (64 // nx), 16), 64 // nx)
    fhalf = pl.ds(c * (nz // 2), nz // 2)
    down = chunks - chunks // 2
    order = [p for k in range(down) for p in (k, down + k) if p < chunks]

    barrier = pltpu.get_barrier_semaphore()
    peers = [{"ctx": (ctx + 1) % nctx}, {"ctx": (ctx + nctx - 1) % nctx}]
    peers += [{"dp": (dp + d) % ndp} for d in range(1, ndp)]
    peers += [{"ctx": ((y + d) % ny) * nz + z} for d in range(1, ny)]
    peers += [{"ctx": y * nz + (z + d) % nz} for d in range(1, nz)]
    for peer in peers:
        pl.semaphore_signal(barrier, inc=1, device_id=peer, device_id_type=pl.DeviceIdType.MESH)

    loads = [
        pltpu.make_async_copy(q_hbm, q_v, lsem.at[0]),
        pltpu.make_async_copy(og_hbm, og_v, lsem.at[1]),
        pltpu.make_async_copy(filt_hbm.at[frows], fin.at[z], lsem.at[2]),
        pltpu.make_async_copy(tab_hbm, tab, lsem.at[3]),
        pltpu.make_async_copy(gv_hbm, gv_v, lsem.at[4]),
    ]
    for load in loads:
        load.start()

    started = []

    def send(src, dst, **where):
        n = len(started)
        copy = pltpu.make_async_remote_copy(
            src_ref=src, dst_ref=dst, send_sem=ssem.at[n], recv_sem=rsem.at[n],
            device_id=where, device_id_type=pl.DeviceIdType.MESH,
        )
        copy.start()
        started.append(copy)
        return copy

    def arrive(copies):
        for copy in copies:
            copy.wait_recv()

    def cols(p, i):
        return pl.ds(pl.multiple_of(i * (nz * 64) + p * 128, 128), 128)

    weight = jnp.where(tok[...] < 4, 1.0, 0.1).astype(F32)
    w_v[...] = jnp.broadcast_to(weight, (rows, rows)).T

    def make_cot(p):
        @pl.loop(0, ny)
        def _(i):
            at = cols(p, i)
            cot[p, i] = (w_v[...] * og_v[:, at].astype(F32) * q_v[:, at].astype(F32)).astype(BF16)

    def hold_gv(p):
        @pl.loop(0, ny)
        def _(i):
            gv_own[p - down, i] = gv_v[:, cols(p, i)]

    def halves(src, dst, to):
        return [(src.at[pl.ds(a * pairs, pairs)], dst.at[pl.ds(a * pairs, pairs)], to) for a in range(2)]

    to_before, to_next = (ctx + nctx - 1) % nctx, (ctx + 1) % nctx

    def halo_halves(p):
        return halves(cot.at[p], halo.at[p], to_before)

    def gv_halves(p):
        return halves(gv_own.at[p - down], gv_in.at[p - down], to_next)

    own, after = pl.ds(0, 2 * rows), pl.ds(2 * rows, 2 * rows)
    back, back_high = pl.ds(4 * rows, 2 * rows), pl.ds(4 * rows, rows)

    def product(wave, other):
        a, b = wave[:rows], wave[rows:]
        e, f = other[:rows], other[rows:]
        return jnp.concatenate([a * e + b * f, b * e - a * f], axis=0)

    def inverse(both):
        top = both.astype(BF16)
        rest = (both - top.astype(F32)).astype(BF16)
        full = mul(tab[back, :], top)
        return full[:rows] + full[rows:] + mul(tab[back_high, :], rest)

    def spectra(p):
        @pl.loop(0, pairs)
        def _(k):
            cspec[p, k] = mul(tab[own, :], twice(jnp.concatenate([cot[p, 2 * k], cot[p, 2 * k + 1]], axis=1)))
            gv = jnp.concatenate([gv_v[:, cols(p, 2 * k)], gv_v[:, cols(p, 2 * k + 1)]], axis=1)
            gspec[p, k] = mul(tab[own, :], twice(gv))

    has_next = jnp.where(ctx == nctx - 1, 0.0, 1.0).astype(F32)
    has_before = jnp.where(ctx == 0, 0.0, 1.0).astype(F32)

    def with_halo(p, k):
        far = mul(tab[after, :], twice(jnp.concatenate([halo[p, 2 * k], halo[p, 2 * k + 1]], axis=1)))
        return cspec[p, k] + has_next * far

    def tap_sums(p):
        @pl.loop(0, pairs)
        def _(k):
            if p < down:
                wave = with_halo(p, k)
                cspec[p, k] = wave
                taps = inverse(product(wave, gspec[p, k]))
            else:
                u = p - down
                far = has_before * mul(tab[after, :], twice(jnp.concatenate([cot[p, 2 * k], cot[p, 2 * k + 1]], axis=1)))
                gv = mul(tab[own, :], twice(jnp.concatenate([gv_in[u, 2 * k], gv_in[u, 2 * k + 1]], axis=1)))
                taps = inverse(product(cspec[p, k], gspec[p, k]) + product(far, gv))
            for h in range(2):
                turned = taps[:, 128 * h:128 * (h + 1)].T
                for zz in range(2):
                    for ci in range(2):
                        at = zz * 64 + ci * 32
                        gst[p, ci, 2 * k + h, zz] = turned[at:at + 32]

    def values(p):
        @pl.loop(0, pairs)
        def _(k):
            f = jnp.concatenate(
                [fbuf[2 * k + h, 2 * p + zz] for h in range(2) for zz in range(2)], axis=0
            )
            fwave = lax.dot_general(
                tab[own, :], jnp.concatenate([f, f], axis=1), (((1,), (1,)), ((), ())),
                preferred_element_type=F32,
            )
            wave = cspec[p, k] if p < down else with_halo(p, k)
            out = inverse(product(wave, fwave)).astype(BF16)
            for h in range(2):
                v_v[:, cols(p, 2 * k + h)] = out[:, 128 * h:128 * (h + 1)]

        stores = []
        for i in range(ny):
            at = cols(p, i)
            stores.append(pltpu.make_async_copy(v_v.at[:, at], v_hbm.at[:, at], osem.at[p, i]))
            stores[-1].start()
        return stores

    def pair_stage(p):
        return [send(gst.at[p, 1 - c], r0.at[p], dp=2 * x + 1 - c)]

    def y_stage(p):
        @pl.loop(0, ny)
        def _(i):
            s0[p, i] = (gst[p, c, i] + r0[p, i]).astype(BF16)

        return [
            send(s0.at[p, (y + d) % ny], r2.at[p, d - 1], ctx=((y + d) % ny) * nz + z)
            for d in range(1, ny)
        ]

    def y_total(p):
        total = gst[p, c, y] + r0[p, y]
        for d in range(1, ny):
            total = total + r2[p, d - 1].astype(F32)
        s2[p] = total

    loads[0].wait()
    loads[1].wait()
    for p in range(chunks):
        make_cot(p)
    loads[4].wait()
    for p in range(down, chunks):
        hold_gv(p)
    loads[2].wait()
    loads[3].wait()
    pl.semaphore_wait(barrier, len(peers))

    fz = [send(fin.at[z], fin.at[z], ctx=y * nz + (z + d) % nz) for d in range(1, nz)]
    down_list = [(p, h) for p in range(chunks) for h in halo_halves(p)]
    up_list = [(p, h) for p in range(down, chunks) for h in gv_halves(p)]
    halos, gvs = {p: [] for p in range(chunks)}, {p: [] for p in range(chunks)}

    def issue(todo, done, n):
        for p, (src, dst, to) in todo[:n]:
            done[p].append(send(src, dst, ctx=to))
        del todo[:n]

    for p in order:
        issue(down_list, halos, 1)
        issue(up_list, gvs, 1)
        spectra(p)

    first, ys, stores = {}, {}, []
    for n, p in enumerate(order):
        arrive(halos[p] if p < down else gvs[p])
        issue(down_list, halos, 1)
        issue(up_list, gvs, 1)
        tap_sums(p)
        first[p] = pair_stage(p)
        if n == 0:
            arrive(fz)
            fy = [
                send(fin.at[fhalf], fbuf.at[y, fhalf, frows], ctx=((y + d) % ny) * nz + z)
                for d in range(1, ny)
            ]
            fbuf[y, fhalf, frows] = fin[fhalf]
        if n >= 1:
            arrive(first[order[n - 1]])
            ys[order[n - 1]] = y_stage(order[n - 1])
        if n == min(1, chunks - 1):
            arrive(fy)
            fx = [
                send(fbuf.at[:, fhalf, frows], fbuf.at[:, fhalf, frows], dp=2 * ((x + d) % nx) + c)
                for d in range(1, nx)
            ]
    arrive(first[order[-1]])
    ys[order[-1]] = y_stage(order[-1])
    issue(down_list, halos, len(down_list))
    arrive(fx)
    fc = [send(fbuf.at[:, fhalf], fbuf.at[:, fhalf], dp=2 * x + 1 - c)]
    for p in range(chunks):
        arrive(ys[p])
        y_total(p)
    zs = []
    for d in range(1, nz):
        zi = (z + d) % nz
        zs.append(send(s2.at[zi // 2, zi % 2], r3.at[d - 1], ctx=y * nz + zi))
    arrive(fc)
    for p in range(down):
        stores += values(p)
    arrive(zs)
    total = s2[z // 2, z % 2]
    for d in range(1, nz):
        total = total + r3[d - 1]
    fg[dp] = total * scale
    ds = [send(fg.at[dp], fg.at[dp], dp=(dp + d) % ndp) for d in range(1, ndp)]
    for p in range(down, chunks):
        arrive(halos[p])
        stores += values(p)
    arrive(ds)
    for ci in range(2):
        total = fg[ci]
        for xi in range(1, nx):
            total = total + fg[2 * xi + ci]
        g_v[ci] = total
    result = pltpu.make_async_copy(g_v, g_hbm, lsem.at[5])
    result.start()
    for copy in started:
        copy.wait_send()
    for store in stores:
        store.wait()
    result.wait()


def body(token_ids, queries, gated_values, out_grad, filters):
    ndp, nctx = lax.axis_size("dp"), lax.axis_size("ctx")
    ny, nz = SIDES[nctx]
    nx = ndp // 2
    _, rows, wide = queries.shape
    assert wide == 64 * nctx and rows == 128
    chunks, pairs = nz // 2, ny // 2
    scale = float(ndp * nctx * rows) ** (-0.5)
    any_space = pl.BlockSpec(memory_space=pl.ANY)
    up = chunks // 2
    remote = chunks * (2 + ny) + 2 * up + 2 * (nz - 1) + (ny - 1) + nx + (ndp - 1)
    value_grad, filter_grad = pl.pallas_call(
        functools.partial(kernel, nx, ny, nz, scale),
        out_shape=(
            jax.ShapeDtypeStruct((rows, wide), BF16),
            jax.ShapeDtypeStruct((2, 32, rows), F32),
        ),
        in_specs=[pl.BlockSpec(memory_space=pltpu.VMEM)] + [any_space] * 5,
        out_specs=(any_space, any_space),
        scratch_shapes=[
            pltpu.VMEM((rows, wide), BF16),
            pltpu.VMEM((rows, wide), BF16),
            pltpu.VMEM((rows, wide), BF16),
            pltpu.VMEM((6 * rows, 2 * rows), BF16),
            pltpu.VMEM((rows, rows), F32),
            pltpu.VMEM((chunks, ny, rows, 128), BF16),
            pltpu.VMEM((chunks, ny, rows, 128), BF16),
            pltpu.VMEM((max(up, 1), ny, rows, 128), BF16),
            pltpu.VMEM((max(up, 1), ny, rows, 128), BF16),
            pltpu.VMEM((chunks, pairs, 2 * rows, 256), F32),
            pltpu.VMEM((chunks, pairs, 2 * rows, 256), F32),
            pltpu.VMEM((nz, 64 // nx, rows), BF16),
            pltpu.VMEM((ny, nz, 64, rows), BF16),
            pltpu.VMEM((rows, wide), BF16),
            pltpu.VMEM((chunks, 2, ny, 2, 32, rows), F32),
            pltpu.VMEM((chunks, ny, 2, 32, rows), F32),
            pltpu.VMEM((chunks, ny, 2, 32, rows), BF16),
            pltpu.VMEM((chunks, ny - 1, 2, 32, rows), BF16),
            pltpu.VMEM((chunks, 2, 32, rows), F32),
            pltpu.VMEM((nz - 1, 32, rows), F32),
            pltpu.VMEM((ndp, 32, rows), F32),
            pltpu.VMEM((2, 32, rows), F32),
            pltpu.SemaphoreType.DMA((6,)),
            pltpu.SemaphoreType.DMA((chunks, ny)),
            pltpu.SemaphoreType.DMA((remote,)),
            pltpu.SemaphoreType.DMA((remote,)),
        ],
        compiler_params=pltpu.CompilerParams(
            collective_id=0, has_side_effects=True, vmem_limit_bytes=60 * 1024 * 1024
        ),
        name="mixer_backward",
    )(
        token_ids, queries[0], gated_values[0], out_grad[0], filters, jnp.asarray(tables(rows)),
    )
    return value_grad[None], filter_grad.reshape(64, rows)


def solution(mesh):
    return jax.shard_map(
        body,
        mesh=mesh,
        in_specs=(
            P("dp", "ctx"),
            P("dp", "ctx", None),
            P("dp", "ctx", None),
            P("dp", "ctx", None),
            P("ctx", None),
        ),
        out_specs=(P("dp", "ctx", None), P("ctx", None)),
        check_vma=False,
    )
```

time: 97.7 us -> 68.1 us (0.70)
  the two profiles are of different devices: /device:TPU:1 before, /device:TPU:9 now
where the time goes in v1:
time: 68.1 us; the launch traced here: 68 us
  Pallas kernels  64.4 us (95%)
  local copies, waits for them, and re-layouts  2.91 us (4%)
    pallas_call x1, Pallas kernels, body(): pl.pallas_call(functools.partial(kernel, nx, ny, nz, scale), out_shape=(j...  64.4 us
    unnamed x4, local copies, waits for them, and re-layouts  2.91 us

profile of v1, /device:TPU:9, one launch (start us, length us, event | category | flops | bytes accessed | tf_op | source)
XLA Modules:
  0.0 68.0 jit_solution(16934988318163181612)
XLA Ops:
  0.6 64.4 %mixer_backward.1 = (bf16[128,4096]{1,0:T(8,128)(2,1)}, f32[2,32,128]{2,1,0:T(8,128)}) custom-call(s32[1,128]{1,0:T(1,128)} %tok.1, bf16[128,4096]{1,0:T(8,128)(2,1)} %bitcast.6, bf16[128,4096]{1,0:T(8,128)(2,1)} %bitcast.7, bf16[128,4096]{1,0:T(8,128)(2,1)} %bitcast.8, bf16[64,128]{1,0:T(8,128)(2,1)} %filt_hbm.1, bf16[768,256]{1,0:T(8,128)(2,1)} %constant.2.clone.tab_hbm), custom_call_target="tpu_custom_call" | custom-call | tf_op jit(solution)/shard_map/mixer_backward/pallas_call | solution.py:305
  65.0 0.0 copy-start
  65.0 2.3 %copy.10 = bf16[1,128,4096]{2,1,0:T(8,128)(2,1)} copy(bf16[1,128,4096]{2,1,0:T(8,128)(2,1)} %bitcast.5) | data formatting | bytes 2097152
  67.3 0.0 copy-done
  67.3 0.6 copy.11
Async XLA Ops:
  65.0 2.3 %copy-start = (f32[2,32,128]{2,1,0:T(8,128)S(1)}, f32[2,32,128]{2,1,0:T(8,128)}, u32[]{:S(2)}) copy-start(f32[2,32,128]{2,1,0:T(8,128)} %get-tuple-element.5) | copy-start | bytes 98308

commit v2 on v1

--- a/solution.py
+++ b/solution.py
@@ -35,9 +35,9 @@
 
 def kernel(
     nx, ny, nz, scale,
-    tok, q_hbm, gv_hbm, og_hbm, filt_hbm, tab_hbm,
+    tok_hbm, q_hbm, gv_hbm, og_hbm, filt_hbm, tab_hbm,
     v_hbm, g_hbm,
-    q_v, og_v, gv_v, tab, w_v, cot, halo, gv_own, gv_in, cspec, gspec, fin, fbuf, v_v,
+    tok, q_v, og_v, gv_v, tab, w_v, cot, halo, gv_own, gv_in, cspec, gspec, fin, fbuf, v_v,
     gst, r0, s0, r2, s2, r3, fg, g_v,
     lsem, osem, ssem, rsem,
 ):
@@ -67,6 +67,7 @@
         pltpu.make_async_copy(filt_hbm.at[frows], fin.at[z], lsem.at[2]),
         pltpu.make_async_copy(tab_hbm, tab, lsem.at[3]),
         pltpu.make_async_copy(gv_hbm, gv_v, lsem.at[4]),
+        pltpu.make_async_copy(tok_hbm, tok, lsem.at[5]),
     ]
     for load in loads:
         load.start()
@@ -90,9 +91,6 @@
     def cols(p, i):
         return pl.ds(pl.multiple_of(i * (nz * 64) + p * 128, 128), 128)
 
-    weight = jnp.where(tok[...] < 4, 1.0, 0.1).astype(F32)
-    w_v[...] = jnp.broadcast_to(weight, (rows, rows)).T
-
     def make_cot(p):
         @pl.loop(0, ny)
         def _(i):
@@ -130,7 +128,7 @@
         return full[:rows] + full[rows:] + mul(tab[back_high, :], rest)
 
     def spectra(p):
-        @pl.loop(0, pairs)
+        @pl.loop(0, pairs, unroll=True)
         def _(k):
             cspec[p, k] = mul(tab[own, :], twice(jnp.concatenate([cot[p, 2 * k], cot[p, 2 * k + 1]], axis=1)))
             gv = jnp.concatenate([gv_v[:, cols(p, 2 * k)], gv_v[:, cols(p, 2 * k + 1)]], axis=1)
@@ -144,7 +142,7 @@
         return cspec[p, k] + has_next * far
 
     def tap_sums(p):
-        @pl.loop(0, pairs)
+        @pl.loop(0, pairs, unroll=True)
         def _(k):
             if p < down:
                 wave = with_halo(p, k)
@@ -163,7 +161,7 @@
                         gst[p, ci, 2 * k + h, zz] = turned[at:at + 32]
 
     def values(p):
-        @pl.loop(0, pairs)
+        @pl.loop(0, pairs, unroll=True)
         def _(k):
             f = jnp.concatenate(
                 [fbuf[2 * k + h, 2 * p + zz] for h in range(2) for zz in range(2)], axis=0
@@ -203,15 +201,15 @@
             total = total + r2[p, d - 1].astype(F32)
         s2[p] = total
 
+    loads[5].wait()
+    weight = jnp.where(tok[...] < 4, 1.0, 0.1).astype(F32)
+    w_v[...] = jnp.broadcast_to(weight, (rows, rows)).T
     loads[0].wait()
     loads[1].wait()
-    for p in range(chunks):
-        make_cot(p)
+    make_cot(0)
     loads[4].wait()
-    for p in range(down, chunks):
-        hold_gv(p)
+    hold_gv(down)
     loads[2].wait()
-    loads[3].wait()
     pl.semaphore_wait(barrier, len(peers))
 
     fz = [send(fin.at[z], fin.at[z], ctx=y * nz + (z + d) % nz) for d in range(1, nz)]
@@ -219,53 +217,77 @@
     up_list = [(p, h) for p in range(down, chunks) for h in gv_halves(p)]
     halos, gvs = {p: [] for p in range(chunks)}, {p: [] for p in range(chunks)}
 
-    def issue(todo, done, n):
-        for p, (src, dst, to) in todo[:n]:
-            done[p].append(send(src, dst, ctx=to))
-        del todo[:n]
-
-    for p in order:
-        issue(down_list, halos, 1)
-        issue(up_list, gvs, 1)
+    ways = ((down_list, halos, []), (up_list, gvs, []))
+    sent = []
+
+    def issue():
+        for todo, done, flight in ways:
+            if todo:
+                p, (src, dst, to) = todo.pop(0)
+                flight.append(send(src, dst, ctx=to))
+                done[p].append(flight[-1])
+
+    def pace():
+        for todo, done, flight in ways:
+            if todo:
+                oldest = flight.pop(0)
+                oldest.wait_send()
+                sent.append(oldest)
+        issue()
+
+    issue()
+    loads[3].wait()
+    spectra(0)
+    issue()
+    for p in range(1, chunks):
+        make_cot(p)
+        if p > down:
+            hold_gv(p)
+    for p in range(1, chunks):
         spectra(p)
+    pace()
+    arrive(fz)
+    fy = [
+        send(fin.at[fhalf], fbuf.at[y, fhalf, frows], ctx=((y + d) % ny) * nz + z)
+        for d in range(1, ny)
+    ]
+    fbuf[y, fhalf, frows] = fin[fhalf]
+    pace()
 
     first, ys, stores = {}, {}, []
     for n, p in enumerate(order):
         arrive(halos[p] if p < down else gvs[p])
-        issue(down_list, halos, 1)
-        issue(up_list, gvs, 1)
         tap_sums(p)
         first[p] = pair_stage(p)
-        if n == 0:
-            arrive(fz)
-            fy = [
-                send(fin.at[fhalf], fbuf.at[y, fhalf, frows], ctx=((y + d) % ny) * nz + z)
-                for d in range(1, ny)
-            ]
-            fbuf[y, fhalf, frows] = fin[fhalf]
-        if n >= 1:
-            arrive(first[order[n - 1]])
-            ys[order[n - 1]] = y_stage(order[n - 1])
-        if n == min(1, chunks - 1):
-            arrive(fy)
-            fx = [
-                send(fbuf.at[:, fhalf, frows], fbuf.at[:, fhalf, frows], dp=2 * ((x + d) % nx) + c)
-                for d in range(1, nx)
-            ]
-    arrive(first[order[-1]])
-    ys[order[-1]] = y_stage(order[-1])
-    issue(down_list, halos, len(down_list))
+        if n % 2:
+            for r in order[n - 1:n + 1]:
+                arrive(first[r])
+                ys[r] = y_stage(r)
+            pace()
+            if n == 1:
+                arrive(fy)
+                fx = [
+                    send(fbuf.at[:, fhalf, frows], fbuf.at[:, fhalf, frows], dp=2 * ((x + d) % nx) + c)
+                    for d in range(1, nx)
+                ]
+            pace()
     arrive(fx)
     fc = [send(fbuf.at[:, fhalf], fbuf.at[:, fhalf], dp=2 * x + 1 - c)]
-    for p in range(chunks):
+    for p in order[:-1]:
         arrive(ys[p])
         y_total(p)
+    arrive(fc)
+    stores += values(0)
+    arrive(ys[order[-1]])
+    y_total(order[-1])
     zs = []
     for d in range(1, nz):
         zi = (z + d) % nz
         zs.append(send(s2.at[zi // 2, zi % 2], r3.at[d - 1], ctx=y * nz + zi))
-    arrive(fc)
-    for p in range(down):
+    for p in range(1, down):
+        stores += values(p)
+    for p in range(down, chunks - 1):
+        arrive(halos[p])
         stores += values(p)
     arrive(zs)
     total = s2[z // 2, z % 2]
@@ -273,19 +295,20 @@
         total = total + r3[d - 1]
     fg[dp] = total * scale
     ds = [send(fg.at[dp], fg.at[dp], dp=(dp + d) % ndp) for d in range(1, ndp)]
-    for p in range(down, chunks):
-        arrive(halos[p])
-        stores += values(p)
+    if chunks > 1:
+        arrive(halos[chunks - 1])
+        stores += values(chunks - 1)
     arrive(ds)
     for ci in range(2):
         total = fg[ci]
         for xi in range(1, nx):
             total = total + fg[2 * xi + ci]
         g_v[ci] = total
-    result = pltpu.make_async_copy(g_v, g_hbm, lsem.at[5])
+    result = pltpu.make_async_copy(g_v, g_hbm, lsem.at[6])
     result.start()
     for copy in started:
-        copy.wait_send()
+        if not any(copy is other for other in sent):
+            copy.wait_send()
     for store in stores:
         store.wait()
     result.wait()
@@ -308,9 +331,10 @@
             jax.ShapeDtypeStruct((rows, wide), BF16),
             jax.ShapeDtypeStruct((2, 32, rows), F32),
         ),
-        in_specs=[pl.BlockSpec(memory_space=pltpu.VMEM)] + [any_space] * 5,
+        in_specs=[any_space] * 6,
         out_specs=(any_space, any_space),
         scratch_shapes=[
+            pltpu.VMEM((1, rows), jnp.int32),
             pltpu.VMEM((rows, wide), BF16),
             pltpu.VMEM((rows, wide), BF16),
             pltpu.VMEM((rows, wide), BF16),
@@ -333,7 +357,7 @@
             pltpu.VMEM((nz - 1, 32, rows), F32),
             pltpu.VMEM((ndp, 32, rows), F32),
             pltpu.VMEM((2, 32, rows), F32),
-            pltpu.SemaphoreType.DMA((6,)),
+            pltpu.SemaphoreType.DMA((7,)),
             pltpu.SemaphoreType.DMA((chunks, ny)),
             pltpu.SemaphoreType.DMA((remote,)),
             pltpu.SemaphoreType.DMA((remote,)),

time: 68.1 us -> 62 us (0.910)
  the two profiles are of different devices: /device:TPU:9 before, /device:TPU:1 now
where the time goes in v2:
time: 62 us; the launch traced here: 61.9 us
  Pallas kernels  58.3 us (94%)
  local copies, waits for them, and re-layouts  2.91 us (5%)
  between operations  0.65 us (1%)
    pallas_call x1, Pallas kernels, body(): pl.pallas_call(functools.partial(kernel, nx, ny, nz, scale), out_shape=(j...  58.3 us
    unnamed x4, local copies, waits for them, and re-layouts  2.91 us

profile of v2, /device:TPU:1, one launch (start us, length us, event | category | flops | bytes accessed | tf_op | source)
XLA Modules:
  0.0 61.9 jit_solution(16200048384354349232)
XLA Ops:
  0.6 58.3 %mixer_backward.1 = (bf16[128,4096]{1,0:T(8,128)(2,1)}, f32[2,32,128]{2,1,0:T(8,128)}) custom-call(s32[1,128]{1,0:T(1,128)} %tok_hbm.1, bf16[128,4096]{1,0:T(8,128)(2,1)} %bitcast.6, bf16[128,4096]{1,0:T(8,128)(2,1)} %bitcast.7, bf16[128,4096]{1,0:T(8,128)(2,1)} %bitcast.8, bf16[64,128]{1,0:T(8,128)(2,1)} %filt_hbm.1, bf16[768,256]{1,0:T(8,128)(2,1)} %constant.2.clone.tab_hbm), custom_call_target="tpu_custom_call" | custom-call | tf_op jit(solution)/shard_map/mixer_backward/pallas_call | solution.py:328
  58.9 0.0 copy-start
  58.9 2.3 %copy.10 = bf16[1,128,4096]{2,1,0:T(8,128)(2,1)} copy(bf16[1,128,4096]{2,1,0:T(8,128)(2,1)} %bitcast.5) | data formatting | bytes 2097152
  61.2 0.0 copy-done
  61.2 0.6 copy.11
Async XLA Ops:
  58.9 2.3 %copy-start = (f32[2,32,128]{2,1,0:T(8,128)S(1)}, f32[2,32,128]{2,1,0:T(8,128)}, u32[]{:S(2)}) copy-start(f32[2,32,128]{2,1,0:T(8,128)} %get-tuple-element.5) | copy-start | bytes 98308

commit v3 on v2

--- a/solution.py
+++ b/solution.py
@@ -38,7 +38,7 @@
     tok_hbm, q_hbm, gv_hbm, og_hbm, filt_hbm, tab_hbm,
     v_hbm, g_hbm,
     tok, q_v, og_v, gv_v, tab, w_v, cot, halo, gv_own, gv_in, cspec, gspec, fin, fbuf, v_v,
-    gst, r0, s0, r2, s2, r3, fg, g_v,
+    gst, r0, s0, r2, s2, sz, r3, fg, g_v,
     lsem, osem, ssem, rsem,
 ):
     rows = q_v.shape[0]
@@ -200,6 +200,7 @@
         for d in range(1, ny):
             total = total + r2[p, d - 1].astype(F32)
         s2[p] = total
+        sz[p] = total.astype(BF16)
 
     loads[5].wait()
     weight = jnp.where(tok[...] < 4, 1.0, 0.1).astype(F32)
@@ -264,27 +265,23 @@
                 arrive(first[r])
                 ys[r] = y_stage(r)
             pace()
-            if n == 1:
-                arrive(fy)
-                fx = [
-                    send(fbuf.at[:, fhalf, frows], fbuf.at[:, fhalf, frows], dp=2 * ((x + d) % nx) + c)
-                    for d in range(1, nx)
-                ]
             pace()
-    arrive(fx)
-    fc = [send(fbuf.at[:, fhalf], fbuf.at[:, fhalf], dp=2 * x + 1 - c)]
-    for p in order[:-1]:
+    arrive(fy)
+    fx = [
+        send(fbuf.at[:, fhalf, frows], fbuf.at[:, fhalf, frows], dp=2 * ((x + d) % nx) + c)
+        for d in range(1, nx)
+    ]
+    for p in order:
         arrive(ys[p])
         y_total(p)
-    arrive(fc)
-    stores += values(0)
-    arrive(ys[order[-1]])
-    y_total(order[-1])
     zs = []
     for d in range(1, nz):
         zi = (z + d) % nz
-        zs.append(send(s2.at[zi // 2, zi % 2], r3.at[d - 1], ctx=y * nz + zi))
-    for p in range(1, down):
+        zs.append(send(sz.at[zi // 2, zi % 2], r3.at[d - 1], ctx=y * nz + zi))
+    arrive(fx)
+    fc = [send(fbuf.at[:, fhalf], fbuf.at[:, fhalf], dp=2 * x + 1 - c)]
+    arrive(fc)
+    for p in range(down):
         stores += values(p)
     for p in range(down, chunks - 1):
         arrive(halos[p])
@@ -292,7 +289,7 @@
     arrive(zs)
     total = s2[z // 2, z % 2]
     for d in range(1, nz):
-        total = total + r3[d - 1]
+        total = total + r3[d - 1].astype(F32)
     fg[dp] = total * scale
     ds = [send(fg.at[dp], fg.at[dp], dp=(dp + d) % ndp) for d in range(1, ndp)]
     if chunks > 1:
@@ -354,7 +351,8 @@
             pltpu.VMEM((chunks, ny, 2, 32, rows), BF16),
             pltpu.VMEM((chunks, ny - 1, 2, 32, rows), BF16),
             pltpu.VMEM((chunks, 2, 32, rows), F32),
-            pltpu.VMEM((nz - 1, 32, rows), F32),
+            pltpu.VMEM((chunks, 2, 32, rows), BF16),
+            pltpu.VMEM((nz - 1, 32, rows), BF16),
             pltpu.VMEM((ndp, 32, rows), F32),
             pltpu.VMEM((2, 32, rows), F32),
             pltpu.SemaphoreType.DMA((7,)),

time: 62 us -> 63.9 us (1.031)
  Pallas kernels: 58.3 us -> 60.2 us
    pallas_call x1, Pallas kernels: 58.3 us -> 60.2 us  [body(): pl.pallas_call(functools.partial(kernel, nx, ny, nz, scale), out_shape=(j...]
where the time goes in v3:
time: 63.9 us; the launch traced here: 63.8 us
  Pallas kernels  60.2 us (94%)
  local copies, waits for them, and re-layouts  2.91 us (5%)
  between operations  0.65 us (1%)
    pallas_call x1, Pallas kernels, body(): pl.pallas_call(functools.partial(kernel, nx, ny, nz, scale), out_shape=(j...  60.2 us
    unnamed x4, local copies, waits for them, and re-layouts  2.91 us

profile of v3, /device:TPU:1, one launch (start us, length us, event | category | flops | bytes accessed | tf_op | source)
XLA Modules:
  0.0 63.8 jit_solution(8168664314687562088)
XLA Ops:
  0.6 60.2 %mixer_backward.1 = (bf16[128,4096]{1,0:T(8,128)(2,1)}, f32[2,32,128]{2,1,0:T(8,128)}) custom-call(s32[1,128]{1,0:T(1,128)} %tok_hbm.1, bf16[128,4096]{1,0:T(8,128)(2,1)} %bitcast.6, bf16[128,4096]{1,0:T(8,128)(2,1)} %bitcast.7, bf16[128,4096]{1,0:T(8,128)(2,1)} %bitcast.8, bf16[64,128]{1,0:T(8,128)(2,1)} %filt_hbm.1, bf16[768,256]{1,0:T(8,128)(2,1)} %constant.2.clone.tab_hbm), custom_call_target="tpu_custom_call" | custom-call | tf_op jit(solution)/shard_map/mixer_backward/pallas_call | solution.py:325
  60.9 0.0 copy-start
  60.9 2.3 %copy.10 = bf16[1,128,4096]{2,1,0:T(8,128)(2,1)} copy(bf16[1,128,4096]{2,1,0:T(8,128)(2,1)} %bitcast.5) | data formatting | bytes 2097152
  63.2 0.0 copy-done
  63.2 0.6 copy.11
Async XLA Ops:
  60.9 2.3 %copy-start = (f32[2,32,128]{2,1,0:T(8,128)S(1)}, f32[2,32,128]{2,1,0:T(8,128)}, u32[]{:S(2)}) copy-start(f32[2,32,128]{2,1,0:T(8,128)} %get-tuple-element.5) | copy-start | bytes 98308
